TPU v7x, 32 devices: a whole 2x2x4 slice. The times are simulated.
32 devices in a mesh: space: 4 (over y, core), tm: 8 (over z, x).
Axes of the slice: x: 2, y: 2, z: 4, core: 2. Of those that a mesh axis runs over, the one named last changes fastest.
Arguments:
- snapshots: bfloat16 [4096, 8192], P('space', 'tm'), may hold values from -6 to 6
- basis: bfloat16 [4096, 64], P('space'), may hold values from -0.09375 to 0.09375
- lengths: int32 [4], replicated, may hold values from 1540 to 2048
Outputs:
- gram_matrix: float32 [2144, 2144], P('space')
- right_sides: float32 [2144, 64], P('space')
Inputs may be any that keep to these rules, and one draw needn't show every extreme that they name: lengths[k] snapshots of trajectory k are recorded; later positions of its slot of 2048 are padding.
All inputs are finite; a program needn't handle non-finite values.
Results may differ from a plain program's by a relative error of at most 0.0003.
Values sent between devices are 32-bit elements; how exact they have to be, the bound alone decides.
A program may use at most 64 MiB of HBM per device.

v0:
```python
import functools

import jax
import jax.numpy as jnp
from jax import lax
from jax.experimental import pallas as pl
from jax.experimental.pallas import tpu as pltpu
from jax.sharding import PartitionSpec as P

LANES = 128
BF16 = jnp.bfloat16
NT = (((1,), (1,)), ((), ()))


def round_up(value, step):
    return -(-value // step) * step


def split(value):
    high = value.astype(BF16)
    return high, (value - high.astype(jnp.float32)).astype(BF16)


def gram_kernel(
    rows, feats, side_at, inv_ref, x_ref, d_ref, gram_ref, side_ref, wide, high, low, row_high, row_low, total
):
    step = pl.program_id(0)
    tiles, modes, _ = x_ref.shape
    start = lax.axis_index("space") * rows
    padded_rows = row_high.shape[0]
    width = high.shape[0]

    @pl.when(step == 0)
    def _():
        total[...] = jnp.zeros_like(total)
        wide[feats:side_at, :] = jnp.zeros((side_at - feats, LANES), jnp.float32)

    for k in range(tiles):
        lanes = slice(k * LANES, (k + 1) * LANES)
        wide[0:modes, :] = x_ref[k]
        at = modes
        for i in range(modes):
            wide[at : at + modes - i, :] = x_ref[k, i : i + 1, :] * x_ref[k, i:modes, :]
            at += modes - i
        wide[side_at:width, :] = d_ref[k]
        high[:, lanes], low[:, lanes] = split(wide[...])
        row_high[:, lanes], row_low[:, lanes] = split(wide[pl.ds(start, padded_rows), :])

    for at in range(0, width, 256):
        cols = slice(at, min(at + 256, width))
        dot = functools.partial(lax.dot_general, dimension_numbers=NT, preferred_element_type=jnp.float32)
        total[:, cols] += (
            dot(row_high[...], high[cols, :])
            + dot(row_high[...], low[cols, :])
            + dot(row_low[...], high[cols, :])
        )

    @pl.when(step == pl.num_programs(0) - 1)
    def _():
        inv = inv_ref[0]
        gram_ref[...] = total[0:rows, 0:feats] * inv
        side_ref[...] = total[0:rows, side_at:width] * inv


def gram(scaled, dscaled, inv_samples, rows, feats):
    tiles, modes, _ = scaled.shape
    per_step = 8
    side_at = round_up(feats, LANES)
    width = side_at + modes
    padded = round_up(rows, 16)
    block = pl.BlockSpec((per_step, modes, LANES), lambda t: (t, 0, 0))
    span = per_step * LANES
    return pl.pallas_call(
        functools.partial(gram_kernel, rows, feats, side_at),
        grid=(tiles // per_step,),
        in_specs=[pl.BlockSpec(memory_space=pltpu.SMEM), block, block],
        out_specs=[
            pl.BlockSpec((rows, feats), lambda t: (0, 0)),
            pl.BlockSpec((rows, modes), lambda t: (0, 0)),
        ],
        out_shape=[
            jax.ShapeDtypeStruct((rows, feats), jnp.float32),
            jax.ShapeDtypeStruct((rows, modes), jnp.float32),
        ],
        scratch_shapes=[
            pltpu.VMEM((width, LANES), jnp.float32),
            pltpu.VMEM((width, span), BF16),
            pltpu.VMEM((width, span), BF16),
            pltpu.VMEM((padded, span), BF16),
            pltpu.VMEM((padded, span), BF16),
            pltpu.VMEM((padded, width), jnp.float32),
        ],
        compiler_params=pltpu.CompilerParams(vmem_limit_bytes=56 * 1024 * 1024),
        cost_estimate=pl.CostEstimate(
            flops=6 * rows * width * tiles * LANES, bytes_accessed=4 * rows * feats, transcendentals=0
        ),
    )(inv_samples.reshape(1), scaled, dscaled)


def shards(snapshots, basis, lengths):
    modes = basis.shape[1]
    feats = modes * (modes + 3) // 2
    horizon = snapshots.shape[1]
    rows = feats // lax.axis_size("space")
    partial = jnp.einsum("cr,ct->rt", basis, snapshots, preferred_element_type=jnp.float32)
    partial = partial.reshape(modes, horizon // LANES, LANES).transpose(1, 0, 2)
    share = lax.psum_scatter(partial, "space", scatter_dimension=0, tiled=True)
    states = lax.all_gather(share, ("tm", "space"), axis=0, tiled=True)
    tiles = states.shape[0]

    before = jnp.pad(states[:-1, :, -2:], ((1, 0), (0, 0), (0, 0)))
    after = jnp.pad(states[1:, :, :2], ((0, 1), (0, 0), (0, 0)))
    wide = jnp.concatenate([before, states, after], axis=2)
    change = (
        wide[:, :, :LANES]
        - 8.0 * wide[:, :, 1 : LANES + 1]
        + 8.0 * wide[:, :, 3 : LANES + 3]
        - wide[:, :, 4:]
    ) / 12.0

    slot = 2 * horizon
    shifted = jnp.arange(tiles * LANES, dtype=jnp.int32) + horizon // 2
    offsets = shifted % slot
    owners = shifted // slot % lengths.shape[0]
    match = owners[:, None] == jnp.arange(lengths.shape[0], dtype=jnp.int32)[None, :]
    limits = jnp.sum(jnp.where(match, lengths[None, :], 0), axis=1)
    living = ((offsets >= 2) & (offsets <= limits - 3)).astype(jnp.float32).reshape(tiles, 1, LANES)
    samples = jnp.sum(lengths - 4).astype(jnp.float32)
    masked = states * living
    energy = jnp.sum(masked * masked, axis=(0, 2))
    inverse = (1.0 / jnp.sqrt(energy / samples + 1e-06))[None, :, None]
    return tuple(gram(masked * inverse, change * living * inverse, 1.0 / samples, rows, feats))


def solution(mesh):
    return jax.shard_map(
        shards,
        mesh=mesh,
        in_specs=(P("space", "tm"), P("space", None), P()),
        out_specs=(P("space", None), P("space", None)),
        check_vma=False,
    )
```

profile of v0, /device:TPU:29, one launch (start us, length us, event | category | flops | bytes accessed | tf_op | source)
XLA Modules:
  0.0 199.3 jit_solution(3925468510663381031)
XLA Ops:
  7.2 0.0 copy-start
  7.2 0.0 copy-start.2
  7.2 0.0 reduce-scatter.2.cloned.1.call-start
  7.2 1.5 copy-done
  8.8 1.4 convolution_bitcast_fusion
  10.2 0.8 copy.12
  11.0 0.0 reduce-scatter.2.cloned.1.call-update
  11.0 0.0 all-gather.2.cloned.1.call-start
  11.0 20.1 %reduce-scatter.2.cloned.1.call-done = f32[2,64,128]{2,1,0:T(8,128)} async-done(((f32[8,64,128]{2,1,0:T(8,128)}), f32[2,64,128]{2,1,0:T(8,128)}) %reduce-scatter.2.cloned.1.call-update) | async-done | bytes 65552 | tf_op jit(solution)/shard_map/reduce_scatter | solution.py:107
  31.1 0.0 all-gather.2.cloned.1.call-update
  31.1 0.0 copy-done.2
  31.2 0.6 add_reduce_fusion
  32.5 0.2 select_reduce_fusion
  32.7 58.4 %all-gather.2.cloned.1.call-done = f32[64,64,128]{2,1,0:T(8,128)} async-done(((f32[2,64,128]{2,1,0:T(8,128)}), f32[64,64,128]{2,1,0:T(8,128)}) %all-gather.2.cloned.1.call-update) | async-done | bytes 2097168 | tf_op jit(solution)/shard_map/all_gather | solution.py:108
  91.1 0.0 copy-start.1
  91.1 2.1 %multiply_reduce_fusion = f32[64]{0:T(128)S(1)} fusion(f32[64,64,128]{2,1,0:T(8,128)} %all-gather.2.cloned.1.call-done, f32[64,128]{1,0:T(8,128)S(1)} %convert_element_type.15), kind=kLoop, calls=%fused_computation.11 | loop fusion | flops 1572800 | bytes 2130176 | tf_op jit(solution)/shard_map/reduce_sum | solution.py:130
  93.2 0.1 copy-done.1
  93.3 0.8 fusion.11
  94.1 1.5 select_maximum_fusion.1
  95.7 3.7 %fusion.1 = (f32[64,64,128]{2,1,0:T(8,128)}, f32[64,64,128]{2,1,0:T(8,128)}) fusion(f32[64,64,130]{2,1,0:T(8,128)S(1)} %get-tuple-element.15, f32[64,64,130]{2,1,0:T(8,128)S(1)} %get-tuple-element.14, f32[64,128]{1,0:T(8,128)S(1)} %get-tuple-element.12, f32[64]{0:T(128)S(1)} %add_rsqrt_fusion, f32[64,64,128]{2,1,0:T(8,128)S(1)} %copy-done.1, ...), kind=kLoop, calls=%fused_computation.6 | loop fusion | flops 4718592 | bytes 14745856 | tf_op jit(solution)/shard_map/mul | solution.py:132
  99.4 91.3 %shard_map.50 = (f32[536,2144]{1,0:T(8,128)}, f32[536,64]{1,0:T(8,128)}) custom-call(f32[1]{0:T(128)} %bitcast.inv_ref, f32[64,64,128]{2,1,0:T(8,128)} %get-tuple-element.19.x_ref, f32[64,64,128]{2,1,0:T(8,128)} %get-tuple-element.18.d_ref), custom_call_target="tpu_custom_call" | custom-call | flops 59013857280 | bytes 4596736 | tf_op jit(solution)/shard_map/pallas_call | solution.py:73
  190.7 1.8 copy.13
  (5 shorter events, 0.1 us)
Async XLA Ops:
  7.2 1.6 copy-start
  7.2 24.0 %copy-start.2 = (s32[4]{0:T(128)S(1)}, s32[4]{0:T(128)}, u32[]{:S(2)}) copy-start(s32[4]{0:T(128)} %param.5) | copy-start | bytes 52
  7.2 23.9 %reduce-scatter.2.cloned.1.call-start = ((), (), s32[]{:S(2)}) async-start(), calls=%async_computation.1 | async-start | bytes 327680 | tf_op jit(solution)/shard_map/reduce_scatter | solution.py:107
  11.0 80.1 %all-gather.2.cloned.1.call-start = ((), (), s32[]{:S(2)}) async-start(), calls=%async_computation.2 | async-start | bytes 2162688 | tf_op jit(solution)/shard_map/all_gather | solution.py:108
  91.1 2.2 %copy-start.1 = (f32[64,64,128]{2,1,0:T(8,128)S(1)}, f32[64,64,128]{2,1,0:T(8,128)}, u32[]{:S(2)}) copy-start(f32[64,64,128]{2,1,0:T(8,128)} %all-gather.2.cloned.1.call-done) | copy-start | bytes 6291460
Sparse Core Ops, SparseCore 0:
  11.1 19.9 reduce-scatter.1
  34.4 56.6 all-gather.1
where the time goes:
time: 202 us; the launch traced here: 199 us
  Pallas kernels  91.3 us (45%)
  waiting for transfers between devices  78.5 us (39%)
  between operations  14.8 us (7%)
  other arithmetic  8.22 us (4%)
  local copies, waits for them, and re-layouts  5.03 us (2%)
    pallas_call x1, Pallas kernels, gram(): pl.pallas_call(functools.partial(gram_kernel, rows, feats, side_at), grid...  91.3 us
    all_gather x1, waiting for transfers between devices, shards(): states = lax.all_gather(share, ('tm', 'space'), axis=0, tiled=True)  58.4 us
    reduce_scatter x1, waiting for transfers between devices, shards(): share = lax.psum_scatter(partial, 'space', scatter_dimension=0, tiled=True)  20.1 us
  transfers between devices with their start and end apart: 2, of which 2 were waited for; matrix products, arithmetic and copies ran while one was open for 0% of the time, Pallas kernels for 0%

commit v1 on v0

v1 whole, which is shorter than its diff:
```python
import functools

import jax
import jax.numpy as jnp
from jax import lax
from jax.experimental import pallas as pl
from jax.experimental.pallas import tpu as pltpu
from jax.sharding import PartitionSpec as P

LANES = 128
BF16 = jnp.bfloat16
F8 = jnp.float8_e5m2
LIFT = 256.0
NT = (((1,), (1,)), ((), ()))


def round_up(value, step):
    return -(-value // step) * step


def split(value):
    high = value.astype(BF16)
    return high, value - high.astype(jnp.float32)


def gather_kernel(part_ref, out_ref, landing, rs_send, rs_recv, tm_send, tm_recv, par_send, par_recv, sib_send, sib_recv):
    spaces, times = lax.axis_size("space"), lax.axis_size("tm")
    s, t = lax.axis_index("space"), lax.axis_index("tm")
    per = landing.shape[1]
    pairs = spaces // 2
    sibling = s + 1 - 2 * lax.rem(s, 2)

    def around(value, step, count):
        return lax.rem(value + step + count, count)

    def block(owner_t, owner_s):
        return out_ref.at[owner_t * spaces + owner_s]

    def remote(src, dst, send, recv, to_s, to_t):
        return pltpu.make_async_remote_copy(
            src_ref=src,
            dst_ref=dst,
            send_sem=send,
            recv_sem=recv,
            device_id=(to_s, to_t),
            device_id_type=pl.DeviceIdType.MESH,
        )

    barrier = pltpu.get_barrier_semaphore()
    for d in range(1, spaces):
        pl.semaphore_signal(
            barrier, inc=1, device_id=(around(s, d, spaces), t), device_id_type=pl.DeviceIdType.MESH
        )
    for d in range(1, times):
        pl.semaphore_signal(
            barrier, inc=1, device_id=(s, around(t, d, times)), device_id_type=pl.DeviceIdType.MESH
        )
    pl.semaphore_wait(barrier, spaces + times - 2)

    sent = []
    first = []
    for d in range(1, spaces):
        to = around(s, d, spaces)
        copy = remote(part_ref.at[pl.ds(to * per, per)], landing.at[d - 1], rs_send.at[d - 1], rs_recv.at[d - 1], to, t)
        copy.start()
        first.append(copy)
    own = part_ref[pl.ds(s * per, per)]
    for d in range(1, spaces):
        first[d - 1].wait_recv()
        own = own + landing[d - 1]
    sent += first
    out_ref[t * spaces + s] = own

    across = []
    for d in range(1, times):
        copy = remote(block(t, s), block(t, s), tm_send.at[d - 1], tm_recv.at[d - 1], s, around(t, d, times))
        copy.start()
        across.append(copy)
    sent += across

    beside = {}
    twins = []
    for d in range(times + 1):
        if d < times:
            src_t = around(t, -d, times)
            if d > 0:
                across[d - 1].wait_recv()
            here = block(src_t, s)
            for e in range(1, pairs):
                at = d * (pairs - 1) + e - 1
                copy = remote(here, here, par_send.at[at], par_recv.at[at], around(s, 2 * e, spaces), t)
                copy.start()
                beside[d, e] = copy
            copy = remote(here, here, sib_send.at[d * pairs], sib_recv.at[d * pairs], sibling, t)
            copy.start()
            twins.append(copy)
        if d > 0:
            src_t = around(t, 1 - d, times)
            for e in range(1, pairs):
                beside[d - 1, e].wait_recv()
                there = block(src_t, around(s, -2 * e, spaces))
                at = (d - 1) * pairs + e
                copy = remote(there, there, sib_send.at[at], sib_recv.at[at], sibling, t)
                copy.start()
                twins.append(copy)
    for copy in twins:
        copy.wait_recv()
    for copy in sent + list(beside.values()) + twins:
        copy.wait_send()


def gathered(part):
    spaces, times = lax.axis_size("space"), lax.axis_size("tm")
    tiles, modes, lanes = part.shape
    per = tiles // spaces
    pairs = spaces // 2
    dma = pltpu.SemaphoreType.DMA
    out = pl.pallas_call(
        gather_kernel,
        in_specs=[pl.BlockSpec(memory_space=pltpu.VMEM)],
        out_specs=pl.BlockSpec(memory_space=pltpu.VMEM),
        out_shape=jax.ShapeDtypeStruct((times * spaces, per, modes, lanes), jnp.float32),
        scratch_shapes=[
            pltpu.VMEM((spaces - 1, per, modes, lanes), jnp.float32),
            dma((spaces - 1,)),
            dma((spaces - 1,)),
            dma((times - 1,)),
            dma((times - 1,)),
            dma((max(1, times * (pairs - 1)),)),
            dma((max(1, times * (pairs - 1)),)),
            dma((times * pairs,)),
            dma((times * pairs,)),
        ],
        compiler_params=pltpu.CompilerParams(
            collective_id=0, has_side_effects=True, vmem_limit_bytes=32 * 1024 * 1024
        ),
    )(part)
    return out.reshape(times * tiles, modes, lanes)


def gram_kernel(
    rows, feats, side_at, inv_ref, x_ref, live_ref, gram_ref, side_ref,
    inverse, scaled, wide, high, low, high8, low8, row_high, row_low, row_high8, row_low8, total
):
    step = pl.program_id(0)
    count, modes, _ = x_ref.shape
    tiles = high.shape[1] // LANES
    start = lax.axis_index("space") * rows
    padded_rows = row_high.shape[0]
    width = high.shape[0]
    whole = high8.shape[0]
    lane = lax.broadcasted_iota(jnp.int32, (modes, LANES), 1)

    @pl.when(step == 0)
    def _():
        total[...] = jnp.zeros_like(total)
        wide[feats:side_at, :] = jnp.zeros((side_at - feats, LANES), jnp.float32)

        def add(k, energy):
            masked = x_ref[k] * live_ref[k]
            return energy + masked * masked

        energy = lax.fori_loop(0, count, add, jnp.zeros((modes, LANES), jnp.float32), unroll=8)
        energy = jnp.sum(energy, axis=1, keepdims=True) * inv_ref[0]
        inverse[...] = jnp.broadcast_to(1.0 / jnp.sqrt(energy + 1e-06), (modes, LANES))

    for k in range(tiles):
        at = step * tiles + k
        lanes = slice(k * LANES, (k + 1) * LANES)
        x = x_ref[at]
        weight = inverse[...] * live_ref[at]
        prev = x_ref[jnp.maximum(at - 1, 0)] * (at > 0).astype(jnp.float32)
        after = x_ref[jnp.minimum(at + 1, count - 1)] * (at < count - 1).astype(jnp.float32)
        back2 = pltpu.roll(jnp.where(lane >= LANES - 2, prev, x), 2, 1)
        back1 = pltpu.roll(jnp.where(lane >= LANES - 1, prev, x), 1, 1)
        ahead1 = pltpu.roll(jnp.where(lane < 1, after, x), LANES - 1, 1)
        ahead2 = pltpu.roll(jnp.where(lane < 2, after, x), LANES - 2, 1)
        change = (back2 - 8.0 * back1 + 8.0 * ahead1 - ahead2) * (1.0 / 12.0)
        scaled[k] = x * weight
        wide[0:modes, :] = x * weight
        wide[side_at:width, :] = change * weight
        at = modes
        for i in range(modes):
            wide[at : at + modes - i, :] = scaled[k, i : i + 1, :] * scaled[k, i:modes, :]
            at += modes - i
        value = wide[...]
        high[:, lanes], rest = split(value)
        low[whole:width, lanes] = rest[whole:width].astype(BF16)
        high8[:, lanes] = value[0:whole].astype(F8)
        low8[:, lanes] = (rest[0:whole] * LIFT).astype(F8)
        value = wide[pl.ds(start, padded_rows), :]
        row_high[:, lanes], rest = split(value)
        row_low[:, lanes] = rest.astype(BF16)
        row_high8[:, lanes] = value.astype(F8)
        row_low8[:, lanes] = (rest * LIFT).astype(F8)

    dot = functools.partial(lax.dot_general, dimension_numbers=NT, preferred_element_type=jnp.float32)
    for at in range(0, whole, 256):
        cols = slice(at, at + 256)
        total[:, cols] += dot(row_high[...], high[cols, :]) + (1.0 / LIFT) * (
            dot(row_high8[...], low8[cols, :]) + dot(row_low8[...], high8[cols, :])
        )
    cols = slice(whole, width)
    total[:, cols] += (
        dot(row_high[...], high[cols, :]) + dot(row_high[...], low[cols, :]) + dot(row_low[...], high[cols, :])
    )

    @pl.when(step == pl.num_programs(0) - 1)
    def _():
        inv = inv_ref[0]
        gram_ref[...] = total[0:rows, 0:feats] * inv
        side_ref[...] = total[0:rows, side_at:width] * inv


def gram(states, living, inv_samples, rows, feats):
    tiles, modes, _ = states.shape
    per_step = 8
    side_at = round_up(feats, LANES)
    width = side_at + modes
    whole = feats // 256 * 256
    padded = round_up(rows, 32)
    span = per_step * LANES
    vmem = pl.BlockSpec(memory_space=pltpu.VMEM)
    return pl.pallas_call(
        functools.partial(gram_kernel, rows, feats, side_at),
        grid=(tiles // per_step,),
        in_specs=[pl.BlockSpec(memory_space=pltpu.SMEM), vmem, vmem],
        out_specs=[
            pl.BlockSpec((rows, feats), lambda t: (0, 0)),
            pl.BlockSpec((rows, modes), lambda t: (0, 0)),
        ],
        out_shape=[
            jax.ShapeDtypeStruct((rows, feats), jnp.float32),
            jax.ShapeDtypeStruct((rows, modes), jnp.float32),
        ],
        scratch_shapes=[
            pltpu.VMEM((modes, LANES), jnp.float32),
            pltpu.VMEM((per_step, modes, LANES), jnp.float32),
            pltpu.VMEM((width, LANES), jnp.float32),
            pltpu.VMEM((width, span), BF16),
            pltpu.VMEM((width, span), BF16),
            pltpu.VMEM((whole, span), F8),
            pltpu.VMEM((whole, span), F8),
            pltpu.VMEM((padded, span), BF16),
            pltpu.VMEM((padded, span), BF16),
            pltpu.VMEM((padded, span), F8),
            pltpu.VMEM((padded, span), F8),
            pltpu.VMEM((padded, width), jnp.float32),
        ],
        compiler_params=pltpu.CompilerParams(vmem_limit_bytes=56 * 1024 * 1024),
        cost_estimate=pl.CostEstimate(
            flops=6 * rows * width * tiles * LANES, bytes_accessed=4 * rows * feats, transcendentals=0
        ),
    )(inv_samples.reshape(1), states, living)


def shards(snapshots, basis, lengths):
    modes = basis.shape[1]
    feats = modes * (modes + 3) // 2
    horizon = snapshots.shape[1]
    rows = feats // lax.axis_size("space")
    partial = jnp.einsum("cr,ct->rt", basis, snapshots, preferred_element_type=jnp.float32)
    partial = partial.reshape(modes, horizon // LANES, LANES).transpose(1, 0, 2)
    states = gathered(partial)
    tiles = states.shape[0]

    slot = 2 * horizon
    shifted = jnp.arange(tiles * LANES, dtype=jnp.int32) + horizon // 2
    offsets = shifted % slot
    owners = shifted // slot % lengths.shape[0]
    match = owners[:, None] == jnp.arange(lengths.shape[0], dtype=jnp.int32)[None, :]
    limits = jnp.sum(jnp.where(match, lengths[None, :], 0), axis=1)
    living = ((offsets >= 2) & (offsets <= limits - 3)).astype(jnp.float32).reshape(tiles, 1, LANES)
    samples = jnp.sum(lengths - 4).astype(jnp.float32)
    return tuple(gram(states, living, 1.0 / samples, rows, feats))


def solution(mesh):
    return jax.shard_map(
        shards,
        mesh=mesh,
        in_specs=(P("space", "tm"), P("space", None), P()),
        out_specs=(P("space", None), P("space", None)),
        check_vma=False,
    )
```

time: 202 us -> 108 us (0.53); the launches traced: 199 us -> 108 us
  waiting for transfers between devices: 78.5 us -> 0 us
  between operations: 14.8 us -> 1.38 us
  Pallas kernels: 91.3 us -> 99.3 us
  other arithmetic: 8.22 us -> 2.95 us
    all_gather x1 -> x0, waiting for transfers between devices: 58.4 us -> none  [shards(): states = lax.all_gather(share, ('tm', 'space'), axis=0, tiled=True)]
    pallas_call x0 -> x1, Pallas kernels: none -> 31.8 us  [gathered(): pl.pallas_call(gather_kernel, in_specs=[pl.BlockSpec(memory_space=pltpu.V...]
    pallas_call x1, Pallas kernels: 91.3 us -> 67.5 us  [gram(): pl.pallas_call(functools.partial(gram_kernel, rows, feats, side_at), grid...]
    reduce_scatter x1 -> x0, waiting for transfers between devices: 20.1 us -> none  [shards(): share = lax.psum_scatter(partial, 'space', scatter_dimension=0, tiled=True)]
    mul x2 -> x0, other arithmetic: 3.77 us -> none  [shards(): change * living * inverse]
    reduce_sum x1 -> x0, other arithmetic: 2.08 us -> none  [shards(): energy = jnp.sum(masked * masked, axis=(0, 2))]
  transfers between devices with their start and end apart: 2 -> 0, of which waited for: 2 -> 0; matrix products, arithmetic and copies ran while one was open for 0% -> 0% of each run, Pallas kernels for 0% -> 0%
where the time goes in v1:
time: 108 us
  Pallas kernels  99.3 us (92%)
  local copies, waits for them, and re-layouts  3.14 us (3%)
  other arithmetic  2.95 us (3%)
  matrix products  1.38 us (1%)
  between operations  1.38 us (1%)
    pallas_call x1, Pallas kernels, gram(): pl.pallas_call(functools.partial(gram_kernel, rows, feats, side_at), grid...  67.5 us
    pallas_call x1, Pallas kernels, gathered(): pl.pallas_call(gather_kernel, in_specs=[pl.BlockSpec(memory_space=pltpu.V...  31.8 us

profile of v1, /device:TPU:29, one launch (start us, length us, event | category | flops | bytes accessed | tf_op | source)
XLA Modules:
  0.0 108.2 jit_solution(14055135506161234492)
XLA Ops:
  0.6 0.0 copy-start
  0.6 1.4 %add_reduce_fusion = s32[]{:T(128)} fusion(s32[4]{0:T(128)} %param.5), kind=kLoop, calls=%fused_computation.23 | loop fusion | flops 7 | bytes 20 | tf_op jit(solution)/shard_map/reduce_sum | solution.py:274
  2.8 0.8 select_reduce_fusion
  3.6 0.7 and_convert_fusion.live_ref
  4.3 0.0 copy-done
  4.3 1.4 %convolution_bitcast_fusion = f32[8,8,8,128]{3,2,1,0:T(8,128)S(1)} fusion(bf16[1024,64]{0,1:T(8,128)(2,1)} %param.4, bf16[1024,1024]{1,0:T(8,128)(2,1)S(1)} %copy-done), kind=kOutput, calls=%fused_computation | convolution fusion | flops 134217728 | bytes 2490368 | tf_op jit(solution)/shard_map/cr,ct->rt/dot_general | solution.py:262
  5.7 31.8 %shard_map.50 = f32[32,2,64,128]{3,2,1,0:T(8,128)S(1)} custom-call(f32[8,64,128]{2,1,0:T(8,128)S(1)} %bitcast.14), custom_call_target="tpu_custom_call" | custom-call | tf_op jit(solution)/shard_map/pallas_call | solution.py:118
  37.5 0.0 copy-start.1
  37.5 1.3 %copy-done.1 = f32[32,2,64,128]{3,2,1,0:T(8,128)} copy-done((f32[32,2,64,128]{3,2,1,0:T(8,128)}, f32[32,2,64,128]{3,2,1,0:T(8,128)S(1)}, u32[]{:S(2)}) %copy-start.1) | copy-done | bytes 2097176
  38.9 67.5 %shard_map.51 = (f32[536,2144]{1,0:T(8,128)}, f32[536,64]{1,0:T(8,128)}) custom-call(f32[1]{0:T(128)} %bitcast.inv_ref, f32[64,64,128]{2,1,0:T(8,128)} %bitcast.13, f32[64,1,128]{2,1,0:T(1,128)} %and_convert_fusion.live_ref), custom_call_target="tpu_custom_call" | custom-call | flops 59013857280 | bytes 4596736 | tf_op jit(solution)/shard_map/pallas_call | solution.py:224
  106.4 1.8 %copy.9 = f32[536,64]{0,1:T(8,128)} copy(f32[536,64]{1,0:T(8,128)} %get-tuple-element.7) | data formatting | bytes 274432 | tf_op jit(solution)/shard_map/pallas_call | solution.py:224
  (3 shorter events, 0.0 us)
Async XLA Ops:
  0.6 3.7 %copy-start = (bf16[1024,1024]{1,0:T(8,128)(2,1)S(1)}, bf16[1024,1024]{1,0:T(8,128)(2,1)}, u32[]{:S(2)}) copy-start(bf16[1024,1024]{1,0:T(8,128)(2,1)} %param.3) | copy-start | bytes 6291460
  37.5 1.4 %copy-start.1 = (f32[32,2,64,128]{3,2,1,0:T(8,128)}, f32[32,2,64,128]{3,2,1,0:T(8,128)S(1)}, u32[]{:S(2)}) copy-start(f32[32,2,64,128]{3,2,1,0:T(8,128)S(1)} %shard_map.50) | copy-start | bytes 6291460

commit v2 on v1

--- a/solution.py
+++ b/solution.py
@@ -139,7 +139,7 @@
 
 
 def gram_kernel(
-    rows, feats, side_at, inv_ref, x_ref, live_ref, gram_ref, side_ref,
+    rows, feats, side_at, horizon, lengths_ref, x_ref, gram_ref, side_ref,
     inverse, scaled, wide, high, low, high8, low8, row_high, row_low, row_high8, row_low8, total
 ):
     step = pl.program_id(0)
@@ -151,24 +151,36 @@
     whole = high8.shape[0]
     lane = lax.broadcasted_iota(jnp.int32, (modes, LANES), 1)
 
+    trajectories = lengths_ref.shape[0]
+    samples = lengths_ref[0] - 4
+    for k in range(1, trajectories):
+        samples = samples + lengths_ref[k] - 4
+    inv = 1.0 / jnp.full((1, 1), samples.astype(jnp.float32))
+
+    def living(at):
+        shifted = at * LANES + horizon // 2
+        limit = lengths_ref[lax.rem(lax.div(shifted, 2 * horizon), trajectories)]
+        offset = lax.rem(shifted, 2 * horizon) + lane
+        return ((offset >= 2) & (offset <= limit - 3)).astype(jnp.float32)
+
     @pl.when(step == 0)
     def _():
         total[...] = jnp.zeros_like(total)
         wide[feats:side_at, :] = jnp.zeros((side_at - feats, LANES), jnp.float32)
 
         def add(k, energy):
-            masked = x_ref[k] * live_ref[k]
+            masked = x_ref[k] * living(k)
             return energy + masked * masked
 
         energy = lax.fori_loop(0, count, add, jnp.zeros((modes, LANES), jnp.float32), unroll=8)
-        energy = jnp.sum(energy, axis=1, keepdims=True) * inv_ref[0]
+        energy = jnp.sum(energy, axis=1, keepdims=True) * inv
         inverse[...] = jnp.broadcast_to(1.0 / jnp.sqrt(energy + 1e-06), (modes, LANES))
 
     for k in range(tiles):
         at = step * tiles + k
         lanes = slice(k * LANES, (k + 1) * LANES)
         x = x_ref[at]
-        weight = inverse[...] * live_ref[at]
+        weight = inverse[...] * living(at)
         prev = x_ref[jnp.maximum(at - 1, 0)] * (at > 0).astype(jnp.float32)
         after = x_ref[jnp.minimum(at + 1, count - 1)] * (at < count - 1).astype(jnp.float32)
         back2 = pltpu.roll(jnp.where(lane >= LANES - 2, prev, x), 2, 1)
@@ -185,7 +197,7 @@
             at += modes - i
         value = wide[...]
         high[:, lanes], rest = split(value)
-        low[whole:width, lanes] = rest[whole:width].astype(BF16)
+        low[:, lanes] = rest[whole:width].astype(BF16)
         high8[:, lanes] = value[0:whole].astype(F8)
         low8[:, lanes] = (rest[0:whole] * LIFT).astype(F8)
         value = wide[pl.ds(start, padded_rows), :]
@@ -202,19 +214,18 @@
         )
     cols = slice(whole, width)
     total[:, cols] += (
-        dot(row_high[...], high[cols, :]) + dot(row_high[...], low[cols, :]) + dot(row_low[...], high[cols, :])
+        dot(row_high[...], high[cols, :]) + dot(row_high[...], low[...]) + dot(row_low[...], high[cols, :])
     )
 
     @pl.when(step == pl.num_programs(0) - 1)
     def _():
-        inv = inv_ref[0]
         gram_ref[...] = total[0:rows, 0:feats] * inv
         side_ref[...] = total[0:rows, side_at:width] * inv
 
 
-def gram(states, living, inv_samples, rows, feats):
+def gram(states, lengths, horizon, rows, feats):
     tiles, modes, _ = states.shape
-    per_step = 8
+    per_step = 16
     side_at = round_up(feats, LANES)
     width = side_at + modes
     whole = feats // 256 * 256
@@ -222,9 +233,9 @@
     span = per_step * LANES
     vmem = pl.BlockSpec(memory_space=pltpu.VMEM)
     return pl.pallas_call(
-        functools.partial(gram_kernel, rows, feats, side_at),
+        functools.partial(gram_kernel, rows, feats, side_at, horizon),
         grid=(tiles // per_step,),
-        in_specs=[pl.BlockSpec(memory_space=pltpu.SMEM), vmem, vmem],
+        in_specs=[pl.BlockSpec(memory_space=pltpu.SMEM), vmem],
         out_specs=[
             pl.BlockSpec((rows, feats), lambda t: (0, 0)),
             pl.BlockSpec((rows, modes), lambda t: (0, 0)),
@@ -238,7 +249,7 @@
             pltpu.VMEM((per_step, modes, LANES), jnp.float32),
             pltpu.VMEM((width, LANES), jnp.float32),
             pltpu.VMEM((width, span), BF16),
-            pltpu.VMEM((width, span), BF16),
+            pltpu.VMEM((width - whole, span), BF16),
             pltpu.VMEM((whole, span), F8),
             pltpu.VMEM((whole, span), F8),
             pltpu.VMEM((padded, span), BF16),
@@ -251,7 +262,7 @@
         cost_estimate=pl.CostEstimate(
             flops=6 * rows * width * tiles * LANES, bytes_accessed=4 * rows * feats, transcendentals=0
         ),
-    )(inv_samples.reshape(1), states, living)
+    )(lengths, states)
 
 
 def shards(snapshots, basis, lengths):
@@ -262,17 +273,7 @@
     partial = jnp.einsum("cr,ct->rt", basis, snapshots, preferred_element_type=jnp.float32)
     partial = partial.reshape(modes, horizon // LANES, LANES).transpose(1, 0, 2)
     states = gathered(partial)
-    tiles = states.shape[0]
-
-    slot = 2 * horizon
-    shifted = jnp.arange(tiles * LANES, dtype=jnp.int32) + horizon // 2
-    offsets = shifted % slot
-    owners = shifted // slot % lengths.shape[0]
-    match = owners[:, None] == jnp.arange(lengths.shape[0], dtype=jnp.int32)[None, :]
-    limits = jnp.sum(jnp.where(match, lengths[None, :], 0), axis=1)
-    living = ((offsets >= 2) & (offsets <= limits - 3)).astype(jnp.float32).reshape(tiles, 1, LANES)
-    samples = jnp.sum(lengths - 4).astype(jnp.float32)
-    return tuple(gram(states, living, 1.0 / samples, rows, feats))
+    return tuple(gram(states, lengths, horizon, rows, feats))
 
 
 def solution(mesh):

time: 108 us -> 105 us (0.972)
  other arithmetic: 2.95 us -> 0 us
  local copies, waits for them, and re-layouts: 3.14 us -> 4.71 us
    reduce_sum x2 -> x0, other arithmetic: 2.25 us -> none  [the longest x1 1.44 us: shards(): samples = jnp.sum(lengths - 4).astype(jnp.float32)]
    unnamed x4, local copies, waits for them, and re-layouts: 1.35 us -> 2.92 us
where the time goes in v2:
time: 105 us
  Pallas kernels  98.5 us (94%)
  local copies, waits for them, and re-layouts  4.71 us (4%)
  matrix products  1.38 us (1%)
    pallas_call x1, Pallas kernels, gram(): pl.pallas_call(functools.partial(gram_kernel, rows, feats, side_at, horiz...  66.7 us
    pallas_call x1, Pallas kernels, gathered(): pl.pallas_call(gather_kernel, in_specs=[pl.BlockSpec(memory_space=pltpu.V...  31.8 us
    unnamed x4, local copies, waits for them, and re-layouts  2.92 us

profile of v2, /device:TPU:29, one launch (start us, length us, event | category | flops | bytes accessed | tf_op | source)
XLA Modules:
  0.0 105.3 jit_solution(5423998176997183966)
XLA Ops:
  0.6 0.0 copy-start
  0.6 1.6 %copy-done = bf16[1024,1024]{1,0:T(8,128)(2,1)S(1)} copy-done((bf16[1024,1024]{1,0:T(8,128)(2,1)S(1)}, bf16[1024,1024]{1,0:T(8,128)(2,1)}, u32[]{:S(2)}) %copy-start) | copy-done | bytes 2097176
  2.2 1.4 %convolution_bitcast_fusion = f32[8,8,8,128]{3,2,1,0:T(8,128)S(1)} fusion(bf16[1024,64]{0,1:T(8,128)(2,1)} %param.4, bf16[1024,1024]{1,0:T(8,128)(2,1)S(1)} %copy-done), kind=kOutput, calls=%fused_computation | convolution fusion | flops 134217728 | bytes 2490368 | tf_op jit(solution)/shard_map/cr,ct->rt/dot_general | solution.py:273
  3.6 31.8 %shard_map.50 = f32[32,2,64,128]{3,2,1,0:T(8,128)S(1)} custom-call(f32[8,64,128]{2,1,0:T(8,128)S(1)} %bitcast.12), custom_call_target="tpu_custom_call" | custom-call | tf_op jit(solution)/shard_map/pallas_call | solution.py:118
  35.4 0.0 copy-start.1
  35.4 1.3 %copy-done.1 = f32[32,2,64,128]{3,2,1,0:T(8,128)} copy-done((f32[32,2,64,128]{3,2,1,0:T(8,128)}, f32[32,2,64,128]{3,2,1,0:T(8,128)S(1)}, u32[]{:S(2)}) %copy-start.1) | copy-done | bytes 2097176
  36.8 66.7 %shard_map.51 = (f32[536,2144]{1,0:T(8,128)}, f32[536,64]{1,0:T(8,128)}) custom-call(s32[4]{0:T(128)} %lengths_ref.1, f32[64,64,128]{2,1,0:T(8,128)} %bitcast.11), custom_call_target="tpu_custom_call" | custom-call | flops 59013857280 | bytes 4596736 | tf_op jit(solution)/shard_map/pallas_call | solution.py:235
  103.5 1.8 %copy.7 = f32[536,64]{0,1:T(8,128)} copy(f32[536,64]{1,0:T(8,128)} %get-tuple-element.5) | data formatting | bytes 274432 | tf_op jit(solution)/shard_map/pallas_call | solution.py:235
  (1 shorter events, 0.0 us)
Async XLA Ops:
  0.6 1.6 %copy-start = (bf16[1024,1024]{1,0:T(8,128)(2,1)S(1)}, bf16[1024,1024]{1,0:T(8,128)(2,1)}, u32[]{:S(2)}) copy-start(bf16[1024,1024]{1,0:T(8,128)(2,1)} %param.3) | copy-start | bytes 6291460
  35.4 1.3 %copy-start.1 = (f32[32,2,64,128]{3,2,1,0:T(8,128)}, f32[32,2,64,128]{3,2,1,0:T(8,128)S(1)}, u32[]{:S(2)}) copy-start(f32[32,2,64,128]{3,2,1,0:T(8,128)S(1)} %shard_map.50) | copy-start | bytes 6291460
